TPU v7x, 128 devices: a whole 4x4x4 slice. The times are simulated.
128 devices in a mesh: gx: 16 (over y, z_hi, core), gy: 8 (over x, z_lo).
Axes of the slice: x: 4, y: 4, z: 4 (z_hi: 2, z_lo: 2; z = z_hi * 2 + z_lo), core: 2. Of those that a mesh axis runs over, the one named last changes fastest.
Arguments:
- magnetic: float32 [3, 32, 512, 4096], P(None, None, 'gy', 'gx'), may hold values from -6 to 6
- register: float32 [3, 32, 512, 4096], P(None, None, 'gy', 'gx'), may hold values from -1.2 to 1.2
- velocity: float32 [3, 8, 128, 1024], P(None, 'gy', 'gx'), may hold values from -6 to 6
- prolong_taps: float32 [3, 4, 3], replicated, may hold values from 0 to 1, as said below
- owner_map: int32 [8], replicated, may hold values from 0 to 7, each once
Outputs:
- new_magnetic: float32 [3, 32, 512, 4096], P(None, None, 'gy', 'gx')
- new_register: float32 [3, 32, 512, 4096], P(None, None, 'gy', 'gx')
Inputs may be any that keep to these rules, and one draw needn't show every extreme that they name: `owner_map`: each of 0 to 7 appears once. `prolong_taps`: along each axis, the three taps of each fine offset are positive and sum to one.
All inputs are finite; a program needn't handle non-finite values.
Results may differ from a plain program's by a relative error of at most 0.0003.
Values sent between devices are 32-bit elements; how exact they have to be, the bound alone decides.
A program may use at most 192 MiB of HBM per device.

v0:
```python
import functools
import math

import jax
import jax.numpy as jnp
from jax import lax
from jax.experimental import pallas as pl
from jax.experimental.pallas import tpu as pltpu
from jax.sharding import PartitionSpec as P

MESH = pl.DeviceIdType.MESH
F32 = jnp.float32
BF16 = jnp.bfloat16

R = 4
LANES = 128
ROWS = 8
UNROLL_BORDER = 8
UNROLL_BASE = 4
UNROLL_BESIDE = 4
UNROLL_CROSS = 2
UNROLL_EDGE = 8
UNROLL_Z = 8
GROUP = 8
OUT = 4
TAIL = 16

alpha_pade = 0.25
coef_pade = 1.5
rk_keep = -5.0 / 9.0
rk_gain = 15.0 / 16.0
reynolds = 10000.0
decay = (-1.0 + math.sqrt(1.0 - 4.0 * alpha_pade * alpha_pade)) / (2.0 * alpha_pade)
scale = coef_pade / 2.0 * (1.0 + decay * decay)


def split(value):
    high = value.astype(BF16)
    low = (value - high.astype(F32)).astype(BF16)
    return high, low


def iota(shape, dim):
    return lax.broadcasted_iota(jnp.int32, shape, dim)


def tap_weights(taps, axis, offset, neighbour):
    out = jnp.zeros(offset.shape, F32)
    for o in range(R):
        for s in range(3):
            out = jnp.where((offset == o) & (neighbour == s), taps[axis, o, s], out)
    return out


def powers(shape, dim, flip):
    index = iota(shape, dim)
    if flip:
        index = shape[dim] - 1 - index
    magnitude = jnp.exp(index.astype(F32) * math.log(abs(decay)))
    return jnp.where((index & 1) == 1, -magnitude, magnitude)


def steps(count, unroll, body, carry):
    def outer(i, carry):
        for k in range(unroll):
            carry = body(i * unroll + k, carry)
        return carry

    return lax.fori_loop(0, count // unroll, outer, carry)


def difference(shape, dim_source, dim_target):
    step = iota(shape, dim_source) - iota(shape, dim_target)
    size = jnp.maximum(jnp.abs(step) - 1, 0)
    magnitude = jnp.exp(size.astype(F32) * math.log(abs(decay)))
    signed = jnp.where((size & 1) == 1, -magnitude, magnitude)
    return jnp.where(step > 0, signed, jnp.where(step < 0, -signed, 0.0))


def dot(a, b):
    return jnp.dot(a, b, preferred_element_type=F32)


def kernel(
    groups_x, groups_y, nu,
    taps_hbm, owner_hbm, mag_hbm, reg_hbm, vel_hbm,
    nm, nr, exr, eyr,
    taps, owner, vel, sv, s1, hs, rv, rh, bxs, bxr, bys, byr, exs, eys,
    px, py, xc, u, ub, dx, dy,
    in_sem, const_sem, vsend, vrecv, wsend, wrecv, hsend, hrecv, bsend, brecv, esend, erecv,
):
    gx, gy = lax.axis_index("gx"), lax.axis_index("gy")
    _, depth, rows, cols = nm.shape
    planes = groups_y

    vel_copy = pltpu.make_async_copy(vel_hbm, vel, const_sem.at[0])
    vel_copy.start()
    taps_copy = pltpu.make_async_copy(taps_hbm, taps, const_sem.at[1])
    owner_copy = pltpu.make_async_copy(owner_hbm, owner, const_sem.at[2])
    taps_copy.start()
    owner_copy.start()
    mag_copies, reg_copies = [], []
    for c in range(3):
        mag_copies.append(pltpu.make_async_copy(mag_hbm.at[c], nm.at[c], in_sem.at[c]))
        reg_copies.append(pltpu.make_async_copy(reg_hbm.at[c], nr.at[c], in_sem.at[3 + c]))
        mag_copies[c].start()
        reg_copies[c].start()

    barrier = pltpu.get_barrier_semaphore()
    x_low, x_high = lax.rem(gx + groups_x - 1, groups_x), lax.rem(gx + 1, groups_x)
    y_low, y_high = lax.rem(gy + groups_y - 1, groups_y), lax.rem(gy + 1, groups_y)
    sides = ((x_low, gy), (x_high, gy), (gx, y_low), (gx, y_high))
    for i in range(1, groups_x):
        pl.semaphore_signal(
            barrier, inc=1, device_id=(lax.rem(gx + i, groups_x), gy), device_id_type=MESH
        )
    for i in range(1, groups_y):
        pl.semaphore_signal(
            barrier, inc=1, device_id=(gx, lax.rem(gy + i, groups_y)), device_id_type=MESH
        )

    vel_copy.wait()
    half_lanes = LANES // 2
    lanes8 = iota((ROWS, LANES), 1)
    row8 = iota((ROWS, LANES), 0)
    tiles = vel.shape[3] // LANES
    flow = [[vel[c, 0, :, m * LANES : (m + 1) * LANES] for m in range(tiles)] for c in range(3)]
    for m in range(tiles):
        turned = [pltpu.roll(flow[c][m], half_lanes, 1) for c in range(3)]
        for odd in range(2):
            first, second, third = (
                (turned[0], flow[1][m], turned[2]) if odd else (flow[0][m], turned[1], flow[2][m])
            )
            sv[2 * m + odd, 0] = jnp.where(lanes8 < half_lanes, first, second)
            tile = jnp.where(lanes8 < half_lanes, third, 0.0)
            for c in range(3):
                if odd:
                    below = flow[c][m][:, half_lanes - 1 : half_lanes]
                    above = flow[c][(m + 1) % tiles][:, 0:1]
                else:
                    below = flow[c][(m - 1) % tiles][:, LANES - 1 : LANES]
                    above = flow[c][m][:, half_lanes : half_lanes + 1]
                tile = jnp.where(lanes8 == half_lanes + c, below, tile)
                tile = jnp.where(lanes8 == half_lanes + 3 + c, above, tile)
            sv[2 * m + odd, 1] = tile
    s1[gx] = sv[gx]

    pl.semaphore_wait(barrier, groups_x + groups_y - 2)

    def send_x(i, _):
        t = lax.rem(gx + i, groups_x)
        pltpu.make_async_remote_copy(
            src_ref=sv.at[t], dst_ref=s1.at[gx], send_sem=vsend, recv_sem=vrecv,
            device_id=(t, gy), device_id_type=MESH,
        ).start()
        return 0

    lax.fori_loop(1, groups_x, send_x, 0)

    taps_copy.wait()
    owner_copy.wait()
    shape = (2 * LANES, cols)
    q, f = iota(shape, 0), iota(shape, 1)
    for c in range(3):
        place = q - c * half_lanes
        place = jnp.where((place >= 0) & (place < half_lanes), place, -100)
        place = jnp.where(q == 3 * half_lanes + c, -1, place)
        place = jnp.where(q == 3 * half_lanes + 3 + c, half_lanes, place)
        px[c, 0], px[c, 1] = split(tap_weights(taps, 0, f & 3, place - (f >> 2) + 1))
    shape = (rows, 12 * ROWS)
    f, q = iota(shape, 0), iota(shape, 1)
    third_part = q >= 8 * ROWS
    q = q & (4 * ROWS - 1)
    place = jnp.where(q < 2 * ROWS, q, -100)
    place = jnp.where((q == 2 * ROWS) | (q == 3 * ROWS + 2), -1, place)
    place = jnp.where((q == 2 * ROWS + 1) | (q == 3 * ROWS + 3), 2 * ROWS, place)
    weights = tap_weights(taps, 1, f & 3, place - (f >> 2) + 1) * (scale * 0.25)
    high = weights.astype(BF16).astype(F32)
    py[...] = jnp.where(third_part, weights - high, high).astype(BF16)
    high, low = split(difference((cols, cols), 0, 1))
    dx[0:cols, :] = high
    dx[cols : 2 * cols, :] = high
    dx[2 * cols : 3 * cols, :] = low
    high, low = split(difference((rows, rows), 1, 0))
    dy[...] = jnp.concatenate([high.astype(F32), high.astype(F32), low.astype(F32)], axis=1).astype(BF16)

    row_of = iota((rows, cols), 0)
    lane_of = iota((rows, cols), 1)
    edge_lane = iota((rows, LANES), 1)

    def base_of(c):
        reg_copies[c].wait()

        def base(z, _):
            b = nm[c, z]
            before = nm[c, lax.rem(z + depth - 1, depth)]
            after = nm[c, lax.rem(z + 1, depth)]
            total = before + after - 6.0 * b
            total = total + jnp.where(row_of == 0, 0.0, pltpu.roll(b, 1, 0))
            total = total + jnp.where(row_of == rows - 1, 0.0, pltpu.roll(b, rows - 1, 0))
            total = total + jnp.where(lane_of == 0, 0.0, pltpu.roll(b, 1, 1))
            total = total + jnp.where(lane_of == cols - 1, 0.0, pltpu.roll(b, cols - 1, 1))
            nr[c, z] = rk_keep * nr[c, z] + nu * total
            return 0

        steps(depth, UNROLL_BASE, base, 0)

    def exchange(xs, xr, ys, yr, ssem, rsem):
        copies = []
        for k in (2, 3, 0, 1):
            src, dst = (xs, xr) if k < 2 else (ys, yr)
            copies.append(
                pltpu.make_async_remote_copy(
                    src_ref=src.at[k % 2], dst_ref=dst.at[1 - k % 2],
                    send_sem=ssem.at[k], recv_sem=rsem.at[k],
                    device_id=sides[k], device_id_type=MESH,
                )
            )
            copies[-1].start()
        return copies

    edges = (jnp.zeros((rows, LANES), F32), jnp.zeros((rows, LANES), F32))
    for c in range(3):
        mag_copies[c].wait()

        def border(z, carry):
            low, high = carry
            bys[0, pl.ds(c * depth + z, 1), :] = nm[c, z, 0:1, :]
            bys[1, pl.ds(c * depth + z, 1), :] = nm[c, z, rows - 1 : rows, :]
            here = edge_lane == c * 32 + z
            low = jnp.where(here, nm[c, z, :, 0:1], low)
            high = jnp.where(here, nm[c, z, :, cols - 1 : cols], high)
            return low, high

        edges = steps(depth, UNROLL_BORDER, border, edges)
    bxs[0], bxs[1] = edges
    b_copies = exchange(bxs, bxr, bys, byr, bsend, brecv)

    base_of(0)

    others = s1.at[pl.ds(0, groups_x - 1)]
    pltpu.make_async_copy(others, others, vrecv).wait()
    for g in range(groups_y):
        below, above = (2 * g - 1) % groups_x, (2 * g + 2) % groups_x
        tile = jnp.zeros((ROWS, LANES), F32)
        for k in range(2):
            tile = jnp.where(row8 == 2 * k, s1[below, k, ROWS - 1 : ROWS, :], tile)
            tile = jnp.where(row8 == 2 * k + 1, s1[above, k, 0:1, :], tile)
        hs[g] = tile
    rv[gy] = s1[pl.ds(2 * gy, 2)]
    rh[gy] = hs[gy]

    def send_y(i, _):
        g = lax.rem(gy + i, groups_y)
        pltpu.make_async_remote_copy(
            src_ref=s1.at[pl.ds(2 * g, 2)], dst_ref=rv.at[gy], send_sem=wsend, recv_sem=wrecv,
            device_id=(gx, g), device_id_type=MESH,
        ).start()
        pltpu.make_async_remote_copy(
            src_ref=hs.at[g], dst_ref=rh.at[gy], send_sem=hsend, recv_sem=hrecv,
            device_id=(gx, g), device_id_type=MESH,
        ).start()
        return 0

    lax.fori_loop(1, groups_y, send_y, 0)

    base_of(1)
    base_of(2)

    for copy in b_copies:
        copy.wait_recv()
    first_row = jnp.where(iota((ROWS, cols), 0) == 0, nu, 0.0)
    last_row = jnp.where(iota((ROWS, cols), 0) == ROWS - 1, nu, 0.0)
    first_lane = jnp.where(iota((1, LANES), 1) == 0, nu, 0.0)
    last_lane = jnp.where(iota((1, LANES), 1) == LANES - 1, nu, 0.0)

    def beside_cells(i, _):
        back = lax.rem(LANES - i * UNROLL_BESIDE, LANES)
        near = [pltpu.roll(bxr[k], back, 1) for k in range(2)]
        for k in range(UNROLL_BESIDE):
            z = i * UNROLL_BESIDE + k
            for c in range(3):
                at = c * 32 + k
                lo = near[0][:, at : at + 1] * first_lane
                hi = near[1][:, at : at + 1] * last_lane
                total = nr[c, z] + jnp.concatenate([lo, hi], axis=1)
                top = byr[0, pl.ds(c * depth + z, 1), :] * first_row
                bottom = byr[1, pl.ds(c * depth + z, 1), :] * last_row
                nr[c, z] = jnp.concatenate(
                    [total[:ROWS] + top, total[ROWS : rows - ROWS], total[rows - ROWS :] + bottom], axis=0
                )
        return 0

    lax.fori_loop(0, depth // UNROLL_BESIDE, beside_cells, 0)

    others = rv.at[pl.ds(0, planes - 1)]
    pltpu.make_async_copy(others, others, wrecv).wait()
    others = rh.at[pl.ds(0, planes - 1)]
    pltpu.make_async_copy(others, others, hrecv).wait()
    main = 2 * ROWS * planes
    blocks = [rv[:, :, k].reshape(main, LANES) for k in range(2)]
    beside = rh[...].reshape(ROWS * planes, LANES)
    blank = jnp.zeros_like(beside)
    coarse = jnp.concatenate(
        [
            jnp.concatenate(blocks, axis=1),
            jnp.concatenate([beside, blank], axis=1),
            jnp.concatenate([blank, beside], axis=1),
        ],
        axis=0,
    )
    high, low = split(coarse)
    for c in range(3):
        xc[c] = dot(high, px[c, 0]) + dot(low, px[c, 0]) + dot(high, px[c, 1])
    for p in range(planes):
        for c in range(3):
            a0 = main + p * ROWS
            b0 = a0 + planes * ROWS
            near = jnp.concatenate(
                [
                    xc[c, p * 2 * ROWS : (p + 1) * 2 * ROWS, :],
                    xc[c, a0 : a0 + ROWS, :],
                    xc[c, b0 : b0 + ROWS, :],
                ],
                axis=0,
            )
            high, low = split(near)
            u[c, p] = dot(py[...], jnp.concatenate([high, low, high], axis=0))

    strip = 2 * ROWS
    lane_low = powers((1, LANES), 1, False)
    lane_high = powers((1, LANES), 1, True)
    sub_low = powers((strip, cols), 0, False)
    sub_high = powers((strip, cols), 0, True)
    strip_lane = iota((strip, LANES), 1)
    weights_z = [[taps[2, o, s] for s in range(3)] for o in range(R)]

    def stored(p):
        at = jnp.int32(0)
        for b in range(planes):
            at = jnp.where(owner[b] == p, b, at)
        return at

    def strips(j, _):
        r0 = pl.multiple_of(j * strip, strip)

        def cross(p, carry):
            low, high = carry
            around = [stored(lax.rem(p + planes + s - 1, planes)) for s in range(3)]
            for o in range(R):
                z = p * R + o
                us = []
                for c in range(3):
                    total = weights_z[o][0] * u[c, around[0], pl.ds(r0, strip), :]
                    total = total + weights_z[o][1] * u[c, around[1], pl.ds(r0, strip), :]
                    us.append(total + weights_z[o][2] * u[c, around[2], pl.ds(r0, strip), :])
                bs = [nm[c, z, pl.ds(r0, strip), :] for c in range(3)]
                for c in range(3):
                    a, b = (c + 1) % 3, (c + 2) % 3
                    e = us[a] * bs[b] - us[b] * bs[a]
                    ub[c, z, pl.ds(r0, strip), :] = e
                    if c > 0:
                        here = strip_lane == (c - 1) * 32 + z
                        sum_low = jnp.sum(e[:, :LANES] * lane_low, axis=1, keepdims=True)
                        sum_high = jnp.sum(e[:, cols - LANES :] * lane_high, axis=1, keepdims=True)
                        low = jnp.where(here, sum_low, low)
                        high = jnp.where(here, sum_high, high)
            return low, high

        zeros = jnp.zeros((strip, LANES), F32)
        low, high = steps(planes, UNROLL_CROSS, cross, (zeros, zeros))
        exs[0, pl.ds(r0, strip), :] = low
        exs[1, pl.ds(r0, strip), :] = high
        return 0

    lax.fori_loop(0, rows // strip, strips, 0)

    def edge(z, _):
        for k, c in enumerate((0, 2)):
            at = pl.ds(k * depth + z, 1)
            eys[0, at, :] = jnp.sum(ub[c, z, 0:strip, :] * sub_low, axis=0, keepdims=True)
            eys[1, at, :] = jnp.sum(ub[c, z, rows - strip : rows, :] * sub_high, axis=0, keepdims=True)
        return 0

    steps(depth, UNROLL_EDGE, edge, 0)
    e_copies = exchange(exs, exr, eys, eyr, esend, erecv)

    warm = TAIL if depth > TAIL else depth
    wrap = 1.0 if depth > TAIL else 1.0 / (1.0 - decay**depth)

    def strips_z(j, _):
        r0 = pl.multiple_of(j * strip, strip)
        part = pl.ds(r0, strip)

        def warm_up(i, carry):
            bx, by, ax, ay = carry
            z = depth - warm + i
            bx = ub[0, z, part, :] + decay * bx
            by = ub[1, z, part, :] + decay * by
            z = warm - 1 - i
            ax = ub[0, z, part, :] + decay * ax
            ay = ub[1, z, part, :] + decay * ay
            return bx, by, ax, ay

        zeros = jnp.zeros((strip, cols), F32)
        carry = steps(warm, UNROLL_Z, warm_up, (zeros,) * 4)
        if wrap != 1.0:
            carry = tuple(wrap * value for value in carry)

        def along_z(i, carry):
            bx, by, ax, ay = carry
            z = i
            nr[1, z, part, :] += -bx
            nr[0, z, part, :] += by
            bx = ub[0, z, part, :] + decay * bx
            by = ub[1, z, part, :] + decay * by
            z = depth - 1 - i
            nr[1, z, part, :] += ax
            nr[0, z, part, :] += -ay
            ax = ub[0, z, part, :] + decay * ax
            ay = ub[1, z, part, :] + decay * ay
            return bx, by, ax, ay

        steps(depth, UNROLL_Z, along_z, carry)
        return 0

    lax.fori_loop(0, rows // strip, strips_z, 0)

    def group(i, _):
        at = pl.ds(i * GROUP, GROUP)
        parts = []
        for c in range(3):
            high, low = split(ub[c, at].reshape(GROUP * rows, cols))
            parts.append((high, low))
        along_x = [
            dot(jnp.concatenate([high, low, high], axis=1), dx[...]).reshape(GROUP, rows, cols)
            for high, low in (parts[1], parts[2])
        ]
        nr[1, at] += -along_x[1]
        for k in range(GROUP):
            z = i * GROUP + k
            cut = slice(k * rows, (k + 1) * rows)
            along_y = [
                dot(dy[...], jnp.concatenate([high[cut], low[cut], high[cut]], axis=0))
                for high, low in (parts[0], parts[2])
            ]
            nr[0, z] += along_y[1]
            nr[2, z] += along_x[0][k] - along_y[0]
        return 0

    lax.fori_loop(0, depth // GROUP, group, 0)

    for copy in e_copies:
        copy.wait_recv()
    for copy in b_copies + e_copies:
        copy.wait_send()
    for ref, sem, count in ((sv, vsend, groups_x), (rv, wsend, groups_y), (rh, hsend, groups_y)):
        part = ref.at[pl.ds(0, count - 1)]
        pltpu.make_async_copy(part, part, sem).wait()


def update_kernel(b, partial, exr, eyr, mag_hbm, reg_hbm, nm, nr, sems):
    _, depth, rows, cols = b.shape
    strip = 2 * ROWS
    lane_low = powers((1, LANES), 1, False)
    lane_high = powers((1, LANES), 1, True)
    sub_low = powers((strip, cols), 0, False)
    sub_high = powers((strip, cols), 0, True)

    def planes(i, _):
        back = lax.rem(LANES - i * OUT, LANES)
        near = [pltpu.roll(exr[k], back, 1) for k in range(2)]
        for k in range(OUT):
            z = i * OUT + k
            for c in range(3):
                total = partial[c, z]
                if c == 1:
                    lo = near[0][:, 32 + k : 33 + k] * lane_low
                    hi = near[1][:, 32 + k : 33 + k] * lane_high
                    total = total + jnp.concatenate([lo, -hi], axis=1)
                if c == 2:
                    lo = near[0][:, k : k + 1] * lane_low
                    hi = near[1][:, k : k + 1] * lane_high
                    total = total - jnp.concatenate([lo, -hi], axis=1)
                if c != 1:
                    at = pl.ds(z if c == 2 else depth + z, 1)
                    top = eyr[0, at, :] * sub_low
                    bottom = eyr[1, at, :] * sub_high
                    first, last = total[:strip], total[rows - strip :]
                    first, last = (first - top, last + bottom) if c == 0 else (first + top, last - bottom)
                    total = jnp.concatenate([first, total[strip : rows - strip], last], axis=0)
                nr[c, z] = total
                nm[c, z] = b[c, z] + rk_gain * total
        at = pl.ds(i * OUT, OUT)
        for c in range(3):
            pltpu.make_async_copy(nr.at[c, at], reg_hbm.at[c, at], sems.at[0]).start()
            pltpu.make_async_copy(nm.at[c, at], mag_hbm.at[c, at], sems.at[1]).start()
        return 0

    lax.fori_loop(0, depth // OUT, planes, 0)
    pltpu.make_async_copy(nr, reg_hbm, sems.at[0]).wait()
    pltpu.make_async_copy(nm, mag_hbm, sems.at[1]).wait()


def body(groups_x, groups_y, magnetic, register, velocity, prolong_taps, owner_map):
    shape = magnetic.shape
    _, depth, rows, cols = shape
    planes = groups_y
    spacing = 2.0 * math.pi / (cols * groups_x)
    nu = 2.0 * math.pi / reynolds / (4.0 * spacing)
    brick = pltpu.VMEM(shape, F32)
    dma = pltpu.SemaphoreType.DMA
    args = [
        pltpu.with_memory_space_constraint(x, pltpu.HBM)
        for x in (prolong_taps, owner_map, magnetic, register, velocity)
    ]
    made = pl.pallas_call(
        functools.partial(kernel, groups_x, groups_y, nu),
        out_shape=(
            brick, brick, pltpu.VMEM((2, rows, LANES), F32), pltpu.VMEM((2, 2 * depth, cols), F32)
        ),
        in_specs=[pl.BlockSpec(memory_space=pltpu.HBM)] * 5,
        out_specs=(pl.BlockSpec(memory_space=pltpu.VMEM),) * 4,
        scratch_shapes=[
            pltpu.SMEM(prolong_taps.shape, F32),
            pltpu.SMEM(owner_map.shape, jnp.int32),
            pltpu.VMEM(velocity.shape, F32),
            pltpu.VMEM((groups_x, 2, ROWS, LANES), F32),
            pltpu.VMEM((groups_x, 2, ROWS, LANES), F32),
            pltpu.VMEM((groups_y, ROWS, LANES), F32),
            pltpu.VMEM((planes, 2, 2, ROWS, LANES), F32),
            pltpu.VMEM((planes, ROWS, LANES), F32),
            pltpu.VMEM((2, rows, LANES), F32),
            pltpu.VMEM((2, rows, LANES), F32),
            pltpu.VMEM((2, 3 * depth, cols), F32),
            pltpu.VMEM((2, 3 * depth, cols), F32),
            pltpu.VMEM((2, rows, LANES), F32),
            pltpu.VMEM((2, 2 * depth, cols), F32),
            pltpu.VMEM((3, 2, 2 * LANES, cols), BF16),
            pltpu.VMEM((rows, 12 * ROWS), BF16),
            pltpu.VMEM((3, 4 * ROWS * planes, cols), F32),
            pltpu.VMEM((3, planes, rows, cols), F32),
            pltpu.VMEM(shape, F32),
            pltpu.VMEM((3 * cols, cols), BF16),
            pltpu.VMEM((rows, 3 * rows), BF16),
            dma((6,)), dma((3,)), dma, dma, dma, dma, dma, dma,
            dma((4,)), dma((4,)), dma((4,)), dma((4,)),
        ],
        compiler_params=pltpu.CompilerParams(
            collective_id=0, has_side_effects=True, vmem_limit_bytes=40 << 20
        ),
    )(*args)
    made = [pltpu.with_memory_space_constraint(x, pltpu.VMEM) for x in made]
    out = jax.ShapeDtypeStruct(shape, F32)
    return pl.pallas_call(
        update_kernel,
        out_shape=(out, out),
        in_specs=[pl.BlockSpec(memory_space=pltpu.VMEM)] * 4,
        out_specs=(pl.BlockSpec(memory_space=pltpu.HBM),) * 2,
        scratch_shapes=[pltpu.VMEM(shape, F32), pltpu.VMEM(shape, F32), dma((2,))],
        compiler_params=pltpu.CompilerParams(vmem_limit_bytes=20 << 20),
    )(*made)


def solution(mesh):
    brick = P(None, None, "gy", "gx")
    return jax.shard_map(
        functools.partial(body, mesh.shape["gx"], mesh.shape["gy"]),
        mesh=mesh,
        in_specs=(brick, brick, P(None, "gy", "gx", None), P(), P()),
        out_specs=(brick, brick),
        check_vma=False,
    )
```

profile of v0, /device:TPU:1, one launch (start us, length us, event | category | flops | bytes accessed | tf_op | source)
XLA Modules:
  0.0 38.3 jit_solution(1270337142312040321)
XLA Ops:
  0.6 32.8 %shard_map.68 = (f32[3,32,64,256]{3,2,1,0:T(8,128)S(1)}, f32[3,32,64,256]{3,2,1,0:T(8,128)S(1)}, f32[2,64,128]{2,1,0:T(8,128)S(1)}, f32[2,64,256]{2,1,0:T(8,128)S(1)}) custom-call(f32[3,4,3]{2,1,0:T(4,128)} %taps_hbm.1, s32[8]{0:T(128)} %owner_hbm.1, f32[3,32,64,256]{3,2,1,0:T(8,128)} %mag_hbm.1, f32[3,32,64,256]{3,2,1,0:T(8,128)} %reg_hbm.1, ...), custom_call_target="tpu_custom_call" | custom-call | tf_op jit(solution)/shard_map/pallas_call | solution.py:517
  33.5 4.8 %shard_map.69 = (f32[3,32,64,256]{3,2,1,0:T(8,128)}, f32[3,32,64,256]{3,2,1,0:T(8,128)}) custom-call(f32[3,32,64,256]{3,2,1,0:T(8,128)S(1)} %get-tuple-element.6.b, f32[3,32,64,256]{3,2,1,0:T(8,128)S(1)} %get-tuple-element.7.partial, f32[2,64,128]{2,1,0:T(8,128)S(1)} %get-tuple-element.8.exr, f32[2,64,256]{2,1,0:T(8,128)S(1)} %get-tuple-element.9.eyr), custom_call_target="tpu_custom_call" | custom-call | tf_op jit(solution)/shard_map/pallas_call | solution.py:555
where the time goes:
time: 38.4 us; the launch traced here: 38.3 us
  Pallas kernels  37.7 us (98%)
  between operations  0.64 us (2%)
    pallas_call x1, Pallas kernels, body(): pl.pallas_call(functools.partial(kernel, groups_x, groups_y, nu), out_sha...  32.8 us
    pallas_call x1, Pallas kernels, body(): pl.pallas_call(update_kernel, out_shape=(out, out), in_specs=[pl.BlockSpe...  4.84 us

commit v1 on v0

--- a/solution.py
+++ b/solution.py
@@ -17,7 +17,6 @@
 ROWS = 8
 UNROLL_BORDER = 8
 UNROLL_BASE = 4
-UNROLL_BESIDE = 4
 UNROLL_CROSS = 2
 UNROLL_EDGE = 8
 UNROLL_Z = 8
@@ -84,9 +83,9 @@
 def kernel(
     groups_x, groups_y, nu,
     taps_hbm, owner_hbm, mag_hbm, reg_hbm, vel_hbm,
-    nm, nr, exr, eyr,
+    nm, nr, exr, eyr, ub, dy,
     taps, owner, vel, sv, s1, hs, rv, rh, bxs, bxr, bys, byr, exs, eys,
-    px, py, xc, u, ub, dx, dy,
+    px, py, xc, u, dx,
     in_sem, const_sem, vsend, vrecv, wsend, wrecv, hsend, hrecv, bsend, brecv, esend, erecv,
 ):
     gx, gy = lax.axis_index("gx"), lax.axis_index("gy")
@@ -110,11 +109,13 @@
     x_low, x_high = lax.rem(gx + groups_x - 1, groups_x), lax.rem(gx + 1, groups_x)
     y_low, y_high = lax.rem(gy + groups_y - 1, groups_y), lax.rem(gy + 1, groups_y)
     sides = ((x_low, gy), (x_high, gy), (gx, y_low), (gx, y_high))
-    for i in range(1, groups_x):
+    far_x = sorted(range(1, groups_x), key=lambda i: abs(i - groups_x // 2))
+    far_y = sorted(range(1, groups_y), key=lambda i: abs(i - groups_y // 2))
+    for i in far_x:
         pl.semaphore_signal(
             barrier, inc=1, device_id=(lax.rem(gx + i, groups_x), gy), device_id_type=MESH
         )
-    for i in range(1, groups_y):
+    for i in far_y:
         pl.semaphore_signal(
             barrier, inc=1, device_id=(gx, lax.rem(gy + i, groups_y)), device_id_type=MESH
         )
@@ -147,15 +148,12 @@
 
     pl.semaphore_wait(barrier, groups_x + groups_y - 2)
 
-    def send_x(i, _):
+    for i in far_x:
         t = lax.rem(gx + i, groups_x)
         pltpu.make_async_remote_copy(
             src_ref=sv.at[t], dst_ref=s1.at[gx], send_sem=vsend, recv_sem=vrecv,
             device_id=(t, gy), device_id_type=MESH,
         ).start()
-        return 0
-
-    lax.fori_loop(1, groups_x, send_x, 0)
 
     taps_copy.wait()
     owner_copy.wait()
@@ -205,9 +203,9 @@
 
         steps(depth, UNROLL_BASE, base, 0)
 
-    def exchange(xs, xr, ys, yr, ssem, rsem):
+    def exchange(xs, xr, ys, yr, ssem, rsem, which=(2, 3, 0, 1)):
         copies = []
-        for k in (2, 3, 0, 1):
+        for k in which:
             src, dst = (xs, xr) if k < 2 else (ys, yr)
             copies.append(
                 pltpu.make_async_remote_copy(
@@ -234,7 +232,6 @@
 
         edges = steps(depth, UNROLL_BORDER, border, edges)
     bxs[0], bxs[1] = edges
-    b_copies = exchange(bxs, bxr, bys, byr, bsend, brecv)
 
     base_of(0)
 
@@ -250,7 +247,7 @@
     rv[gy] = s1[pl.ds(2 * gy, 2)]
     rh[gy] = hs[gy]
 
-    def send_y(i, _):
+    for i in far_y:
         g = lax.rem(gy + i, groups_y)
         pltpu.make_async_remote_copy(
             src_ref=s1.at[pl.ds(2 * g, 2)], dst_ref=rv.at[gy], send_sem=wsend, recv_sem=wrecv,
@@ -260,38 +257,10 @@
             src_ref=hs.at[g], dst_ref=rh.at[gy], send_sem=hsend, recv_sem=hrecv,
             device_id=(gx, g), device_id_type=MESH,
         ).start()
-        return 0
-
-    lax.fori_loop(1, groups_y, send_y, 0)
-
+
+    b_copies = exchange(bxs, bxr, bys, byr, bsend, brecv)
     base_of(1)
     base_of(2)
-
-    for copy in b_copies:
-        copy.wait_recv()
-    first_row = jnp.where(iota((ROWS, cols), 0) == 0, nu, 0.0)
-    last_row = jnp.where(iota((ROWS, cols), 0) == ROWS - 1, nu, 0.0)
-    first_lane = jnp.where(iota((1, LANES), 1) == 0, nu, 0.0)
-    last_lane = jnp.where(iota((1, LANES), 1) == LANES - 1, nu, 0.0)
-
-    def beside_cells(i, _):
-        back = lax.rem(LANES - i * UNROLL_BESIDE, LANES)
-        near = [pltpu.roll(bxr[k], back, 1) for k in range(2)]
-        for k in range(UNROLL_BESIDE):
-            z = i * UNROLL_BESIDE + k
-            for c in range(3):
-                at = c * 32 + k
-                lo = near[0][:, at : at + 1] * first_lane
-                hi = near[1][:, at : at + 1] * last_lane
-                total = nr[c, z] + jnp.concatenate([lo, hi], axis=1)
-                top = byr[0, pl.ds(c * depth + z, 1), :] * first_row
-                bottom = byr[1, pl.ds(c * depth + z, 1), :] * last_row
-                nr[c, z] = jnp.concatenate(
-                    [total[:ROWS] + top, total[ROWS : rows - ROWS], total[rows - ROWS :] + bottom], axis=0
-                )
-        return 0
-
-    lax.fori_loop(0, depth // UNROLL_BESIDE, beside_cells, 0)
 
     others = rv.at[pl.ds(0, planes - 1)]
     pltpu.make_async_copy(others, others, wrecv).wait()
@@ -332,8 +301,7 @@
     lane_high = powers((1, LANES), 1, True)
     sub_low = powers((strip, cols), 0, False)
     sub_high = powers((strip, cols), 0, True)
-    strip_lane = iota((strip, LANES), 1)
-    weights_z = [[taps[2, o, s] for s in range(3)] for o in range(R)]
+    weights_z = [[taps[2, o, n] for n in range(3)] for o in range(R)]
 
     def stored(p):
         at = jnp.int32(0)
@@ -342,38 +310,39 @@
         return at
 
     def strips(j, _):
-        r0 = pl.multiple_of(j * strip, strip)
+        part = pl.ds(pl.multiple_of(j * ROWS, ROWS), ROWS)
 
         def cross(p, carry):
             low, high = carry
-            around = [stored(lax.rem(p + planes + s - 1, planes)) for s in range(3)]
+            around = [stored(lax.rem(p + planes + n - 1, planes)) for n in range(3)]
+            near = [[u[c, around[n], part, :] for n in range(3)] for c in range(3)]
             for o in range(R):
                 z = p * R + o
                 us = []
                 for c in range(3):
-                    total = weights_z[o][0] * u[c, around[0], pl.ds(r0, strip), :]
-                    total = total + weights_z[o][1] * u[c, around[1], pl.ds(r0, strip), :]
-                    us.append(total + weights_z[o][2] * u[c, around[2], pl.ds(r0, strip), :])
-                bs = [nm[c, z, pl.ds(r0, strip), :] for c in range(3)]
+                    total = weights_z[o][0] * near[c][0] + weights_z[o][1] * near[c][1]
+                    us.append(total + weights_z[o][2] * near[c][2])
+                bs = [nm[c, z, part, :] for c in range(3)]
                 for c in range(3):
                     a, b = (c + 1) % 3, (c + 2) % 3
                     e = us[a] * bs[b] - us[b] * bs[a]
-                    ub[c, z, pl.ds(r0, strip), :] = e
+                    ub[c, z, part, :] = e
                     if c > 0:
-                        here = strip_lane == (c - 1) * 32 + z
+                        here = lanes8 == (c - 1) * 32 + z
                         sum_low = jnp.sum(e[:, :LANES] * lane_low, axis=1, keepdims=True)
                         sum_high = jnp.sum(e[:, cols - LANES :] * lane_high, axis=1, keepdims=True)
                         low = jnp.where(here, sum_low, low)
                         high = jnp.where(here, sum_high, high)
             return low, high
 
-        zeros = jnp.zeros((strip, LANES), F32)
+        zeros = jnp.zeros((ROWS, LANES), F32)
         low, high = steps(planes, UNROLL_CROSS, cross, (zeros, zeros))
-        exs[0, pl.ds(r0, strip), :] = low
-        exs[1, pl.ds(r0, strip), :] = high
+        exs[0, part, :] = low
+        exs[1, part, :] = high
         return 0
 
-    lax.fori_loop(0, rows // strip, strips, 0)
+    count = rows // ROWS
+    lax.fori_loop(0, 4, lambda k, _: strips(k + (count - 4) * (k // 2), 0), 0)
 
     def edge(z, _):
         for k, c in enumerate((0, 2)):
@@ -383,7 +352,9 @@
         return 0
 
     steps(depth, UNROLL_EDGE, edge, 0)
-    e_copies = exchange(exs, exr, eys, eyr, esend, erecv)
+    e_copies = exchange(exs, exr, eys, eyr, esend, erecv, (2, 3))
+    lax.fori_loop(2, count - 2, strips, 0)
+    e_copies = e_copies + exchange(exs, exr, eys, eyr, esend, erecv, (0, 1))
 
     warm = TAIL if depth > TAIL else depth
     wrap = 1.0 if depth > TAIL else 1.0 / (1.0 - decay**depth)
@@ -426,26 +397,38 @@
 
     lax.fori_loop(0, rows // strip, strips_z, 0)
 
+    first_row = jnp.where(iota((ROWS, cols), 0) == 0, nu, 0.0)
+    last_row = jnp.where(iota((ROWS, cols), 0) == ROWS - 1, nu, 0.0)
+    first_lane = jnp.where(iota((1, LANES), 1) == 0, nu, 0.0)
+    last_lane = jnp.where(iota((1, LANES), 1) == LANES - 1, nu, 0.0)
+    for copy in b_copies:
+        copy.wait_recv()
+
     def group(i, _):
         at = pl.ds(i * GROUP, GROUP)
-        parts = []
-        for c in range(3):
+        back = lax.rem(LANES - i * GROUP, LANES)
+        near = [pltpu.roll(bxr[k], back, 1) for k in range(2)]
+        along_x = []
+        for c in (1, 2):
             high, low = split(ub[c, at].reshape(GROUP * rows, cols))
-            parts.append((high, low))
-        along_x = [
-            dot(jnp.concatenate([high, low, high], axis=1), dx[...]).reshape(GROUP, rows, cols)
-            for high, low in (parts[1], parts[2])
-        ]
-        nr[1, at] += -along_x[1]
+            out = dot(jnp.concatenate([high, low, high], axis=1), dx[...])
+            along_x.append(out.reshape(GROUP, rows, cols))
         for k in range(GROUP):
             z = i * GROUP + k
-            cut = slice(k * rows, (k + 1) * rows)
-            along_y = [
-                dot(dy[...], jnp.concatenate([high[cut], low[cut], high[cut]], axis=0))
-                for high, low in (parts[0], parts[2])
-            ]
-            nr[0, z] += along_y[1]
-            nr[2, z] += along_x[0][k] - along_y[0]
+            for c in range(3):
+                spot = c * 32 + k
+                lo = near[0][:, spot : spot + 1] * first_lane
+                hi = near[1][:, spot : spot + 1] * last_lane
+                total = nr[c, z] + jnp.concatenate([lo, hi], axis=1)
+                if c == 1:
+                    total = total - along_x[1][k]
+                if c == 2:
+                    total = total + along_x[0][k]
+                top = byr[0, pl.ds(c * depth + z, 1), :] * first_row
+                bottom = byr[1, pl.ds(c * depth + z, 1), :] * last_row
+                nr[c, z] = jnp.concatenate(
+                    [total[:ROWS] + top, total[ROWS : rows - ROWS], total[rows - ROWS :] + bottom], axis=0
+                )
         return 0
 
     lax.fori_loop(0, depth // GROUP, group, 0)
@@ -459,7 +442,7 @@
         pltpu.make_async_copy(part, part, sem).wait()
 
 
-def update_kernel(b, partial, exr, eyr, mag_hbm, reg_hbm, nm, nr, sems):
+def update_kernel(b, partial, exr, eyr, ub, dy, mag_hbm, reg_hbm, nm, nr, sems):
     _, depth, rows, cols = b.shape
     strip = 2 * ROWS
     lane_low = powers((1, LANES), 1, False)
@@ -474,6 +457,10 @@
             z = i * OUT + k
             for c in range(3):
                 total = partial[c, z]
+                if c != 1:
+                    high, low = split(ub[2 - c, z])
+                    out = dot(dy[...], jnp.concatenate([high, low, high], axis=0))
+                    total = total + out if c == 0 else total - out
                 if c == 1:
                     lo = near[0][:, 32 + k : 33 + k] * lane_low
                     hi = near[1][:, 32 + k : 33 + k] * lane_high
@@ -517,10 +504,11 @@
     made = pl.pallas_call(
         functools.partial(kernel, groups_x, groups_y, nu),
         out_shape=(
-            brick, brick, pltpu.VMEM((2, rows, LANES), F32), pltpu.VMEM((2, 2 * depth, cols), F32)
+            brick, brick, pltpu.VMEM((2, rows, LANES), F32), pltpu.VMEM((2, 2 * depth, cols), F32),
+            brick, pltpu.VMEM((rows, 3 * rows), BF16),
         ),
         in_specs=[pl.BlockSpec(memory_space=pltpu.HBM)] * 5,
-        out_specs=(pl.BlockSpec(memory_space=pltpu.VMEM),) * 4,
+        out_specs=(pl.BlockSpec(memory_space=pltpu.VMEM),) * 6,
         scratch_shapes=[
             pltpu.SMEM(prolong_taps.shape, F32),
             pltpu.SMEM(owner_map.shape, jnp.int32),
@@ -540,9 +528,7 @@
             pltpu.VMEM((rows, 12 * ROWS), BF16),
             pltpu.VMEM((3, 4 * ROWS * planes, cols), F32),
             pltpu.VMEM((3, planes, rows, cols), F32),
-            pltpu.VMEM(shape, F32),
             pltpu.VMEM((3 * cols, cols), BF16),
-            pltpu.VMEM((rows, 3 * rows), BF16),
             dma((6,)), dma((3,)), dma, dma, dma, dma, dma, dma,
             dma((4,)), dma((4,)), dma((4,)), dma((4,)),
         ],
@@ -555,7 +541,7 @@
     return pl.pallas_call(
         update_kernel,
         out_shape=(out, out),
-        in_specs=[pl.BlockSpec(memory_space=pltpu.VMEM)] * 4,
+        in_specs=[pl.BlockSpec(memory_space=pltpu.VMEM)] * 6,
         out_specs=(pl.BlockSpec(memory_space=pltpu.HBM),) * 2,
         scratch_shapes=[pltpu.VMEM(shape, F32), pltpu.VMEM(shape, F32), dma((2,))],
         compiler_params=pltpu.CompilerParams(vmem_limit_bytes=20 << 20),

time: 38.4 us -> 35.4 us (0.922); the launches traced: 38.3 us -> 34.9 us
  Pallas kernels: 37.7 us -> 34.3 us
    pallas_call x1, Pallas kernels: 32.8 us -> 29.4 us  [body(): pl.pallas_call(functools.partial(kernel, groups_x, groups_y, nu), out_sha...]
where the time goes in v1:
time: 35.4 us; the launch traced here: 34.9 us
  Pallas kernels  34.3 us (97%)
  between operations  0.64 us (2%)
    pallas_call x1, Pallas kernels, body(): pl.pallas_call(functools.partial(kernel, groups_x, groups_y, nu), out_sha...  29.4 us
    pallas_call x1, Pallas kernels, body(): pl.pallas_call(update_kernel, out_shape=(out, out), in_specs=[pl.BlockSpe...  4.86 us

profile of v1, /device:TPU:1, one launch (start us, length us, event | category | flops | bytes accessed | tf_op | source)
XLA Modules:
  0.0 34.9 jit_solution(8127761371388054946)
XLA Ops:
  0.6 29.4 %shard_map.68 = (f32[3,32,64,256]{3,2,1,0:T(8,128)S(1)}, f32[3,32,64,256]{3,2,1,0:T(8,128)S(1)}, f32[2,64,128]{2,1,0:T(8,128)S(1)}, f32[2,64,256]{2,1,0:T(8,128)...) custom-call(f32[3,4,3]{2,1,0:T(4,128)} %taps_hbm.1, s32[8]{0:T(128)} %owner_hbm.1, ...), custom_call_target="tpu_custom_call" | custom-call | tf_op jit(solution)/shard_map/pallas_call | solution.py:504
  30.1 4.9 %shard_map.69 = (f32[3,32,64,256]{3,2,1,0:T(8,128)}, f32[3,32,64,256]{3,2,1,0:T(8,128)}) custom-call(f32[3,32,64,256]{3,2,1,0:T(8,128)S(1)} %get-tuple-element.8.b, f32[3,32,64,256]{3,2,1,0:T(8,128)S(1)} %get-tuple-element.9.partial, f32[2,64,128]{2,1,0:T(8,128)S(1)} %get-tuple-element.10.exr, f32[2,64,256]{2,1,0:T(8,128)S(1)} %get-tuple-element.11.eyr, ...), custom_call_target="tpu_custom_call" | custom-call | tf_op jit(solution)/shard_map/pallas_call | solution.py:541

commit v2 on v1

--- a/solution.py
+++ b/solution.py
@@ -17,7 +17,7 @@
 ROWS = 8
 UNROLL_BORDER = 8
 UNROLL_BASE = 4
-UNROLL_CROSS = 2
+UNROLL_CROSS = 8
 UNROLL_EDGE = 8
 UNROLL_Z = 8
 GROUP = 8

time: 35.4 us -> 33.3 us (0.941); the launches traced: 34.9 us -> 33.2 us
  Pallas kernels: 34.3 us -> 32.6 us
    pallas_call x1, Pallas kernels: 29.4 us -> 27.7 us  [body(): pl.pallas_call(functools.partial(kernel, groups_x, groups_y, nu), out_sha...]
where the time goes in v2:
time: 33.3 us; the launch traced here: 33.2 us
  Pallas kernels  32.6 us (98%)
  between operations  0.64 us (2%)
    pallas_call x1, Pallas kernels, body(): pl.pallas_call(functools.partial(kernel, groups_x, groups_y, nu), out_sha...  27.7 us
    pallas_call x1, Pallas kernels, body(): pl.pallas_call(update_kernel, out_shape=(out, out), in_specs=[pl.BlockSpe...  4.86 us

profile of v2, /device:TPU:1, one launch (start us, length us, event | category | flops | bytes accessed | tf_op | source)
XLA Modules:
  0.0 33.2 jit_solution(14683934481898887552)
XLA Ops:
  0.6 27.7 %shard_map.68 = (f32[3,32,64,256]{3,2,1,0:T(8,128)S(1)}, f32[3,32,64,256]{3,2,1,0:T(8,128)S(1)}, f32[2,64,128]{2,1,0:T(8,128)S(1)}, f32[2,64,256]{2,1,0:T(8,128)...) custom-call(f32[3,4,3]{2,1,0:T(4,128)} %taps_hbm.1, s32[8]{0:T(128)} %owner_hbm.1, ...), custom_call_target="tpu_custom_call" | custom-call | tf_op jit(solution)/shard_map/pallas_call | solution.py:504
  28.4 4.9 %shard_map.69 = (f32[3,32,64,256]{3,2,1,0:T(8,128)}, f32[3,32,64,256]{3,2,1,0:T(8,128)}) custom-call(f32[3,32,64,256]{3,2,1,0:T(8,128)S(1)} %get-tuple-element.8.b, f32[3,32,64,256]{3,2,1,0:T(8,128)S(1)} %get-tuple-element.9.partial, f32[2,64,128]{2,1,0:T(8,128)S(1)} %get-tuple-element.10.exr, f32[2,64,256]{2,1,0:T(8,128)S(1)} %get-tuple-element.11.eyr, ...), custom_call_target="tpu_custom_call" | custom-call | tf_op jit(solution)/shard_map/pallas_call | solution.py:541
